TPU v7x, 128 devices: a whole 4x4x4 slice. The times are simulated.
128 devices in a mesh: mesh: 32 (over x, z, core), grp: 4 (over y).
Axes of the slice: x: 4, y: 4, z: 4, core: 2. Of those that a mesh axis runs over, the one named last changes fastest.
Arguments:
- forcing: float32 [32, 524288], P(None, ('mesh', 'grp')), may hold values from -134 to 134
- plan: int32 [128, 64], P(('mesh', 'grp')), may hold values from 0 to 63, each once within a row
- lower_blocks: float32 [256, 458752], P(None, ('mesh', 'grp')), may hold values from -0.25 to 0.25
- lower_columns: int32 [7168, 4], P(('mesh', 'grp')), may hold values from 0 to 15
- upper_blocks: float32 [256, 458752], P(None, ('mesh', 'grp')), may hold values from -0.25 to 0.25
- upper_columns: int32 [7168, 4], P(('mesh', 'grp')), may hold values from 0 to 15
- diag_blocks: float32 [64, 524288], P(None, ('mesh', 'grp')), may hold values from -0.5 to 4.5
- inverse_blocks: float32 [64, 524288], P(None, ('mesh', 'grp')), may hold values from -0.1 to 0.75
- halo_list: int32 [1024, 4], P(('mesh', 'grp')), may hold values from 0 to 7
Outputs:
- basis: float32 [32, 524288], P(None, ('mesh', 'grp'))
- adjoint_field: float32 [32, 524288], P(None, ('mesh', 'grp'))
Inputs may be any that keep to these rules, and one draw needn't show every extreme that they name: Each row of plan is a permutation of 0 to 63.
All inputs are finite; a program needn't handle non-finite values.
Results may differ from a plain program's by a relative error of at most 0.00011.
Values sent between devices are 32-bit elements; how exact they have to be, the bound alone decides.
No kernel may reach another device: no remote copies, remote signals or barrier semaphores. Data moves between devices by JAX's collectives and lax.ppermute only.
A program may use at most 128 MiB of HBM per device.

v0:
```python
import math

import jax
import jax.numpy as jnp
from jax import lax
from jax.sharding import PartitionSpec as P

BLOCK = 64
KL = 4
KU = 4
LEV = 8
RPL = 8
HB = 4
NB = 64


HIGH = lax.Precision.HIGHEST


def extended_2(cells, sides, width):
    for axis, dim in sides:
        count = lax.axis_size(axis)
        ends = count - 1
        head = lax.slice_in_dim(cells, 0, width, axis=dim)
        tail = lax.slice_in_dim(cells, cells.shape[dim] - width, cells.shape[dim], axis=dim)
        cells = jnp.concatenate(
            [
                lax.ppermute(tail, axis, [(i, (i + 1) % count) for i in range(ends)]),
                cells,
                lax.ppermute(head, axis, [((i + 1) % count, i) for i in range(ends)]),
            ],
            axis=dim,
        )
    return cells


def shifted(block, axis, distance):
    devices = range(lax.axis_size(axis))
    route = [(i - distance, i) for i in devices if i - distance in devices]
    return lax.ppermute(block, axis, route)


def diagonal_product(blocks, values):
    return jnp.einsum("sjc,cjr->sjr", values, blocks, precision=HIGH)


def diagonal_transposed(blocks, values):
    return jnp.einsum("sjr,cjr->sjc", values, blocks, precision=HIGH)


def block_product(slots, columns, blocks):
    picked = slots[:, columns]
    picked = picked.reshape(picked.shape[0], picked.shape[1], -1)
    return jnp.einsum("sjq,qjr->sjr", picked, blocks, precision=HIGH)


def level_slots(source, rows):
    chosen = source[:, rows].reshape(source.shape[0], -1)
    width = chosen.shape[1]
    extended = extended_2(chosen, ((("mesh", "grp"), 1),), width)
    lower_side = extended[:, :width].reshape(source.shape[0], HB, BLOCK)
    higher_side = extended[:, 2 * width :].reshape(source.shape[0], HB, BLOCK)
    return jnp.concatenate([source, lower_side, higher_side], axis=1)


def push_terms(values, columns, blocks, rows):
    terms = jnp.einsum("sjr,qjr->sjq", values, blocks, precision=HIGH)
    terms = terms.reshape(terms.shape[0], terms.shape[1], columns.shape[1], BLOCK)
    slots = jnp.zeros((values.shape[0], RPL + 2 * HB, BLOCK), jnp.float32).at[:, columns].add(terms)
    toward_lower = slots[:, RPL : RPL + HB].reshape(values.shape[0], -1)
    toward_higher = slots[:, RPL + HB :].reshape(values.shape[0], -1)
    from_higher = shifted(toward_lower, ("mesh", "grp"), -1)
    from_lower = shifted(toward_higher, ("mesh", "grp"), 1)
    arriving = (from_higher + from_lower).reshape(values.shape[0], HB, BLOCK)
    return slots[:, :RPL].at[:, rows].add(arriving)


def precondition(right, lower, lower_index, upper, upper_index, inverse, halo):
    forward = []
    for level in range(LEV):
        term = right[level]
        if level > 0:
            slots = level_slots(forward[level - 1], halo[level - 1])
            term = term - block_product(slots, lower_index[level - 1], lower[:, level - 1])
        forward.append(diagonal_product(inverse[:, level], term))
    result = [None] * LEV
    result[LEV - 1] = forward[LEV - 1]
    for level in range(LEV - 2, -1, -1):
        slots = level_slots(result[level + 1], halo[level + 1])
        term = block_product(slots, upper_index[level], upper[:, level])
        result[level] = forward[level] - diagonal_product(inverse[:, level], term)
    return result


def operate(field, diagonal, lower, lower_index, upper, upper_index, halo):
    stacked = jnp.stack(field, axis=1)
    columns = stacked.shape[0]
    level_rows = jnp.arange(LEV)[:, None]
    chosen = stacked[:, level_rows, halo].reshape(columns, LEV, -1)
    width = chosen.shape[2]
    extended = extended_2(chosen, ((("mesh", "grp"), 2),), width)
    lower_side = extended[:, :, :width].reshape(columns, LEV, HB, BLOCK)
    higher_side = extended[:, :, 2 * width :].reshape(columns, LEV, HB, BLOCK)
    slots = jnp.concatenate([stacked, lower_side, higher_side], axis=2)
    image = []
    for level in range(LEV):
        term = diagonal_product(diagonal[:, level], field[level])
        if level > 0:
            term = term + block_product(
                slots[:, level - 1], lower_index[level - 1], lower[:, level - 1]
            )
        if level < LEV - 1:
            term = term + block_product(slots[:, level + 1], upper_index[level], upper[:, level])
        image.append(term)
    return image


def adjoint(source, lower, lower_index, upper, upper_index, inverse, halo):
    before = [None] * LEV
    after = [None] * LEV
    before[0] = source[0]
    after[0] = diagonal_transposed(inverse[:, 0], before[0])
    for level in range(LEV - 1):
        incoming = push_terms(after[level], upper_index[level], upper[:, level], halo[level + 1])
        before[level + 1] = source[level + 1] - incoming
        after[level + 1] = diagonal_transposed(inverse[:, level + 1], before[level + 1])
    result = [None] * LEV
    result[LEV - 1] = diagonal_transposed(inverse[:, LEV - 1], before[LEV - 1])
    for level in range(LEV - 2, -1, -1):
        incoming = push_terms(result[level + 1], lower_index[level], lower[:, level], halo[level])
        result[level] = diagonal_transposed(inverse[:, level], before[level] - incoming)
    return result


def into_levels(matrix, order):
    blocks = matrix.reshape(matrix.shape[0], -1, BLOCK)[:, order]
    blocks = blocks.reshape(matrix.shape[0], LEV, RPL, BLOCK)
    return [blocks[:, level] for level in range(LEV)]


def out_of_levels(levels, order):
    stacked = jnp.stack(levels, axis=1).reshape(levels[0].shape[0], -1, BLOCK)
    natural = jnp.zeros_like(stacked).at[:, order].set(stacked)
    return natural.reshape(levels[0].shape[0], -1)


def whole_orthonormal(sketch):
    for repeat in range(2):
        gram = lax.psum(jnp.dot(sketch, sketch.T, precision=HIGH), ("mesh", "grp"))
        factor = jnp.linalg.cholesky(gram)
        sketch = jax.scipy.linalg.solve_triangular(factor, sketch, lower=True)
    return sketch


def shards(
    forcing,
    plan,
    lower_blocks,
    lower_columns,
    upper_blocks,
    upper_columns,
    diag_blocks,
    inverse_blocks,
    halo_list,
):
    order = plan.reshape(-1)
    lower = lower_blocks.reshape(KL * BLOCK, LEV - 1, RPL, BLOCK)
    upper = upper_blocks.reshape(KU * BLOCK, LEV - 1, RPL, BLOCK)
    lower_index = lower_columns.reshape(LEV - 1, RPL, KL)
    upper_index = upper_columns.reshape(LEV - 1, RPL, KU)
    diagonal = diag_blocks.reshape(BLOCK, LEV, RPL, BLOCK)
    inverse = inverse_blocks.reshape(BLOCK, LEV, RPL, BLOCK)
    right = into_levels(forcing, order)
    first = precondition(right, lower, lower_index, upper, upper_index, inverse, halo_list)
    image = operate(first, diagonal, lower, lower_index, upper, upper_index, halo_list)
    residual = [right[level] - image[level] for level in range(LEV)]
    second = precondition(residual, lower, lower_index, upper, upper_index, inverse, halo_list)
    sketch = out_of_levels([first[level] + second[level] for level in range(LEV)], order)
    scale = math.sqrt(NB * BLOCK * lax.axis_size("mesh") * lax.axis_size("grp"))
    ortho = whole_orthonormal(sketch)
    basis = scale * ortho
    result = adjoint(
        into_levels(basis, order), lower, lower_index, upper, upper_index, inverse, halo_list
    )
    return (basis, out_of_levels(result, order))


def solution(mesh):
    in_specs = (
        P(None, ("mesh", "grp")),
        P(("mesh", "grp"), None),
        P(None, ("mesh", "grp")),
        P(("mesh", "grp"), None),
        P(None, ("mesh", "grp")),
        P(("mesh", "grp"), None),
        P(None, ("mesh", "grp")),
        P(None, ("mesh", "grp")),
        P(("mesh", "grp"), None),
    )
    out_specs = (P(None, ("mesh", "grp")), P(None, ("mesh", "grp")))
    return jax.shard_map(shards, mesh=mesh, in_specs=in_specs, out_specs=out_specs, check_vma=False)
```

profile of v0, /device:TPU:2, one launch (start us, length us, event | category | flops | bytes accessed | tf_op | source)
XLA Modules:
  0.0 1333.8 jit_solution(1439101605135765562)
XLA Ops:
  12.5 3.5 collective-permute-start
  16.0 6.3 collective-permute-start.1
  34.2 5.1 copy.531
  51.4 7.9 collective-permute-start.3
  73.5 7.9 collective-permute-start.5
  96.2 8.3 collective-permute-start.7
  118.6 7.9 collective-permute-start.9
  142.2 7.9 collective-permute-start.11
  164.3 7.9 collective-permute-start.13
  187.3 7.9 collective-permute-start.15
  195.2 5.2 copy.581
  210.7 8.0 collective-permute-start.17
  230.7 7.9 collective-permute-start.19
  252.1 7.9 collective-permute-start.21
  275.0 7.9 collective-permute-start.23
  302.5 7.9 collective-permute-start.25
  336.5 8.1 collective-permute-start.27
  379.1 7.9 collective-permute-start.29
  413.1 8.3 collective-permute-start.31
  511.8 8.0 collective-permute-start.33
  552.5 7.9 collective-permute-start.35
  592.1 7.9 collective-permute-start.37
  631.8 8.1 collective-permute-start.39
  661.8 7.9 collective-permute-start.41
  687.5 7.9 collective-permute-start.43
  705.9 7.9 collective-permute-start.45
  722.6 8.3 collective-permute-start.47
  739.3 7.9 collective-permute-start.49
  755.9 7.9 collective-permute-start.51
  772.6 7.9 collective-permute-start.53
  789.2 7.9 collective-permute-start.55
  806.0 8.0 collective-permute-start.57
  828.5 6.2 scatter_fusion
  837.3 66.8 %psum.14 = f32[32,32]{0,1:T(8,128)S(1)} all-reduce(f32[32,32]{0,1:T(8,128)S(1)} %convolution_bitcast_fusion.79), channel_id=1, replica_groups=mesh['mesh'=32,'grp'=4] {'mesh','grp'}, use_global_device_ids=true, to_apply=%region_1.0 | all-reduce | flops 1024 | bytes 8192 | tf_op jit(solution)/shard_map/psum | solution.py:149
  913.7 63.5 %psum.15 = f32[32,32]{0,1:T(8,128)S(1)} all-reduce(f32[32,32]{0,1:T(8,128)S(1)} %fusion.179), channel_id=1, replica_groups=mesh['mesh'=32,'grp'=4] {'mesh','grp'}, use_global_device_ids=true, to_apply=%region_4.0 | all-reduce | flops 1024 | bytes 8192 | tf_op jit(solution)/shard_map/psum | solution.py:149
  999.6 4.5 collective-permute-start.58
  1006.9 7.7 collective-permute-done.59
  1032.3 3.9 collective-permute-start.61
  1036.9 5.1 collective-permute-done.61
  1061.9 3.9 collective-permute-start.63
  1066.5 5.1 collective-permute-done.63
  1092.1 3.9 collective-permute-start.65
  1096.7 5.1 collective-permute-done.65
  1121.9 3.9 collective-permute-start.67
  1126.5 5.1 collective-permute-done.67
  1151.6 3.9 collective-permute-start.69
  1156.2 5.1 collective-permute-done.69
  1181.3 3.9 collective-permute-start.71
  1185.9 5.1 collective-permute-done.71
  1205.9 3.9 collective-permute-start.73
  1209.8 5.5 collective-permute-done.73
  1226.1 4.1 collective-permute-start.75
  1230.2 5.3 collective-permute-done.75
  1244.5 3.9 collective-permute-start.77
  1248.4 5.5 collective-permute-done.77
  1262.3 3.9 collective-permute-start.79
  1266.2 5.5 collective-permute-done.79
  1280.0 3.9 collective-permute-start.81
  1284.0 5.5 collective-permute-done.81
  1296.7 3.9 collective-permute-start.83
  1300.7 5.5 collective-permute-done.83
  1313.6 3.9 collective-permute-start.85
  1317.5 5.5 collective-permute-done.85
  1325.7 6.2 scatter_fusion.29
  (1106 shorter events, 811.3 us)
Async XLA Ops:
  12.5 27.5 %collective-permute-start = (f32[32,256]{1,0:T(8,128)S(1)}, f32[32,256]{1,0:T(8,128)S(1)}, u32[]{:S(2)}, u32[]{:S(2)}) collective-permute-start(f32[32,256]{1,0:T(8,128)S(1)} %reshape.894), channel_id=1, source_target_pairs={{0,1},{1,2},{2,3},{3,4},{4,5},{5,6},{6,7},{7,8},{8,9},{9,10},{10,1... | collective-permute-start | bytes 98312 | tf_op jit(solution)/shard_map/ppermute | solution.py:28
  16.0 24.7 %collective-permute-start.1 = (f32[32,256]{1,0:T(8,128)S(1)}, f32[32,256]{1,0:T(8,128)S(1)}, u32[]{:S(2)}, u32[]{:S(2)}) collective-permute-start(f32[32,256]{1,0:T(8,128)S(1)} %reshape.894), channel_id=1, source_target_pairs={{1,0},{2,1},{3,2},{4,3},{5,4},{6,5},{7,6},{8,7},{9,8},{10,9},{11,1... | collective-permute-start | bytes 98312 | tf_op jit(solution)/shard_map/ppermute | solution.py:30
  49.5 12.4 collective-permute-start.2
  51.4 11.2 collective-permute-start.3
  71.6 12.4 collective-permute-start.4
  73.5 11.9 collective-permute-start.5
  94.3 12.8 collective-permute-start.6
  96.2 11.7 collective-permute-start.7
  116.7 13.2 collective-permute-start.8
  118.6 12.8 collective-permute-start.9
  140.3 12.6 collective-permute-start.10
  142.2 11.4 collective-permute-start.11
  162.4 12.6 collective-permute-start.12
  164.3 12.1 collective-permute-start.13
  185.4 15.2 %collective-permute-start.14 = (f32[32,256]{1,0:T(8,128)S(1)}, f32[32,256]{1,0:T(8,128)S(1)}, u32[]{:S(2)}, u32[]{:S(2)}) collective-permute-start(f32[32,256]{1,0:T(8,128)S(1)} %reshape.923), channel_id=1, source_target_pairs={{0,1},{1,2},{2,3},{3,4},{4,5},{5,6},{6,7},{7,8},{8,9},{9,10},{10,1... | collective-permute-start | bytes 98312 | tf_op jit(solution)/shard_map/ppermute | solution.py:28
  187.3 13.4 %collective-permute-start.15 = (f32[32,256]{1,0:T(8,128)S(1)}, f32[32,256]{1,0:T(8,128)S(1)}, u32[]{:S(2)}, u32[]{:S(2)}) collective-permute-start(f32[32,256]{1,0:T(8,128)S(1)} %reshape.923), channel_id=1, source_target_pairs={{1,0},{2,1},{3,2},{4,3},{5,4},{6,5},{7,6},{8,7},{9,8},{10,9},{11,1... | collective-permute-start | bytes 98312 | tf_op jit(solution)/shard_map/ppermute | solution.py:30
  208.8 11.9 collective-permute-start.16
  210.7 10.1 collective-permute-start.17
  228.8 11.7 collective-permute-start.18
  230.7 10.6 collective-permute-start.19
  250.2 11.8 collective-permute-start.20
  252.1 10.6 collective-permute-start.21
  273.1 11.8 collective-permute-start.22
  275.0 9.9 collective-permute-start.23
  300.5 11.8 collective-permute-start.24
  302.5 12.8 collective-permute-start.25
  334.6 12.0 collective-permute-start.26
  336.5 13.0 collective-permute-start.27
  377.2 12.8 collective-permute-start.28
  379.1 13.1 collective-permute-start.29
  411.2 77.0 %collective-permute-start.30 = (f32[32,256]{1,0:T(8,128)}, f32[32,256]{1,0:T(8,128)}, u32[]{:S(2)}, u32[]{:S(2)}) collective-permute-start(f32[32,256]{1,0:T(8,128)} %reshape.959), channel_id=1, source_target_pairs={{0,1},{1,2},{2,3},{3,4},{4,5},{5,6},{6,7},{7,8},{8,9},{9,10},{10,1... | collective-permute-start | bytes 98312 | tf_op jit(solution)/shard_map/ppermute | solution.py:28
  413.1 78.1 %collective-permute-start.31 = (f32[32,256]{1,0:T(8,128)}, f32[32,256]{1,0:T(8,128)}, u32[]{:S(2)}, u32[]{:S(2)}) collective-permute-start(f32[32,256]{1,0:T(8,128)} %reshape.959), channel_id=1, source_target_pairs={{1,0},{2,1},{3,2},{4,3},{5,4},{6,5},{7,6},{8,7},{9,8},{10,9},{11,1... | collective-permute-start | bytes 98312 | tf_op jit(solution)/shard_map/ppermute | solution.py:30
  509.9 19.1 %collective-permute-start.32 = (f32[32,256]{1,0:T(8,128)}, f32[32,256]{1,0:T(8,128)}, u32[]{:S(2)}, u32[]{:S(2)}) collective-permute-start(f32[32,256]{1,0:T(8,128)} %reshape.965), channel_id=1, source_target_pairs={{0,1},{1,2},{2,3},{3,4},{4,5},{5,6},{6,7},{7,8},{8,9},{9,10},{10,1... | collective-permute-start | bytes 98312 | tf_op jit(solution)/shard_map/ppermute | solution.py:28
  511.8 20.1 %collective-permute-start.33 = (f32[32,256]{1,0:T(8,128)}, f32[32,256]{1,0:T(8,128)}, u32[]{:S(2)}, u32[]{:S(2)}) collective-permute-start(f32[32,256]{1,0:T(8,128)} %reshape.965), channel_id=1, source_target_pairs={{1,0},{2,1},{3,2},{4,3},{5,4},{6,5},{7,6},{8,7},{9,8},{10,9},{11,1... | collective-permute-start | bytes 98312 | tf_op jit(solution)/shard_map/ppermute | solution.py:30
  550.6 18.0 %collective-permute-start.34 = (f32[32,256]{1,0:T(8,128)}, f32[32,256]{1,0:T(8,128)}, u32[]{:S(2)}, u32[]{:S(2)}) collective-permute-start(f32[32,256]{1,0:T(8,128)} %reshape.971), channel_id=1, source_target_pairs={{0,1},{1,2},{2,3},{3,4},{4,5},{5,6},{6,7},{7,8},{8,9},{9,10},{10,1... | collective-permute-start | bytes 98312 | tf_op jit(solution)/shard_map/ppermute | solution.py:28
  552.5 19.0 %collective-permute-start.35 = (f32[32,256]{1,0:T(8,128)}, f32[32,256]{1,0:T(8,128)}, u32[]{:S(2)}, u32[]{:S(2)}) collective-permute-start(f32[32,256]{1,0:T(8,128)} %reshape.971), channel_id=1, source_target_pairs={{1,0},{2,1},{3,2},{4,3},{5,4},{6,5},{7,6},{8,7},{9,8},{10,9},{11,1... | collective-permute-start | bytes 98312 | tf_op jit(solution)/shard_map/ppermute | solution.py:30
  590.2 18.0 %collective-permute-start.36 = (f32[32,256]{1,0:T(8,128)}, f32[32,256]{1,0:T(8,128)}, u32[]{:S(2)}, u32[]{:S(2)}) collective-permute-start(f32[32,256]{1,0:T(8,128)} %reshape.977), channel_id=1, source_target_pairs={{0,1},{1,2},{2,3},{3,4},{4,5},{5,6},{6,7},{7,8},{8,9},{9,10},{10,1... | collective-permute-start | bytes 98312 | tf_op jit(solution)/shard_map/ppermute | solution.py:28
  592.1 19.0 %collective-permute-start.37 = (f32[32,256]{1,0:T(8,128)}, f32[32,256]{1,0:T(8,128)}, u32[]{:S(2)}, u32[]{:S(2)}) collective-permute-start(f32[32,256]{1,0:T(8,128)} %reshape.977), channel_id=1, source_target_pairs={{1,0},{2,1},{3,2},{4,3},{5,4},{6,5},{7,6},{8,7},{9,8},{10,9},{11,1... | collective-permute-start | bytes 98312 | tf_op jit(solution)/shard_map/ppermute | solution.py:30
  629.9 18.2 %collective-permute-start.38 = (f32[32,256]{1,0:T(8,128)}, f32[32,256]{1,0:T(8,128)}, u32[]{:S(2)}, u32[]{:S(2)}) collective-permute-start(f32[32,256]{1,0:T(8,128)} %reshape.983), channel_id=1, source_target_pairs={{0,1},{1,2},{2,3},{3,4},{4,5},{5,6},{6,7},{7,8},{8,9},{9,10},{10,1... | collective-permute-start | bytes 98312 | tf_op jit(solution)/shard_map/ppermute | solution.py:28
  631.8 17.7 %collective-permute-start.39 = (f32[32,256]{1,0:T(8,128)}, f32[32,256]{1,0:T(8,128)}, u32[]{:S(2)}, u32[]{:S(2)}) collective-permute-start(f32[32,256]{1,0:T(8,128)} %reshape.983), channel_id=1, source_target_pairs={{1,0},{2,1},{3,2},{4,3},{5,4},{6,5},{7,6},{8,7},{9,8},{10,9},{11,1... | collective-permute-start | bytes 98312 | tf_op jit(solution)/shard_map/ppermute | solution.py:30
  659.9 16.1 %collective-permute-start.40 = (f32[32,256]{1,0:T(8,128)}, f32[32,256]{1,0:T(8,128)}, u32[]{:S(2)}, u32[]{:S(2)}) collective-permute-start(f32[32,256]{1,0:T(8,128)} %reshape.989), channel_id=1, source_target_pairs={{0,1},{1,2},{2,3},{3,4},{4,5},{5,6},{6,7},{7,8},{8,9},{9,10},{10,1... | collective-permute-start | bytes 98312 | tf_op jit(solution)/shard_map/ppermute | solution.py:28
  661.8 15.1 %collective-permute-start.41 = (f32[32,256]{1,0:T(8,128)}, f32[32,256]{1,0:T(8,128)}, u32[]{:S(2)}, u32[]{:S(2)}) collective-permute-start(f32[32,256]{1,0:T(8,128)} %reshape.989), channel_id=1, source_target_pairs={{1,0},{2,1},{3,2},{4,3},{5,4},{6,5},{7,6},{8,7},{9,8},{10,9},{11,1... | collective-permute-start | bytes 98312 | tf_op jit(solution)/shard_map/ppermute | solution.py:30
  685.6 12.2 collective-permute-start.42
  687.5 11.1 collective-permute-start.43
  704.0 9.8 collective-permute-start.44
  720.7 10.2 collective-permute-start.46
  737.4 9.8 collective-permute-start.48
  754.0 9.8 collective-permute-start.50
  770.7 9.8 collective-permute-start.52
  787.3 9.8 collective-permute-start.54
  804.1 10.0 collective-permute-start.56
  1004.8 9.8 collective-permute-start.59
  1027.4 9.6 collective-permute-start.60
  1032.3 9.7 collective-permute-start.61
  1057.0 9.6 collective-permute-start.62
  1061.9 9.7 collective-permute-start.63
  1086.7 10.0 collective-permute-start.64
  1092.1 9.7 collective-permute-start.65
  1116.9 9.6 collective-permute-start.66
  1121.9 9.7 collective-permute-start.67
  1146.6 9.6 collective-permute-start.68
  1151.6 9.7 collective-permute-start.69
  1176.3 9.6 collective-permute-start.70
  1181.3 9.7 collective-permute-start.71
  (131 other events, 2772.7 us)
where the time goes:
time: 1360 us; the launch traced here: 1330 us
  local copies, waits for them, and re-layouts  467 us (34%)
  starting transfers between devices  368 us (27%)
  matrix products  161 us (12%)
  blocking collectives  130 us (10%)
  other arithmetic  116 us (9%)
  waiting for transfers between devices  86.2 us (6%)
    ppermute x29, starting transfers between devices, extended_2(): lax.ppermute(head, axis, [((i + 1) % count, i) for i in range(ends)])  229 us
    gather x84, local copies, waits for them, and re-layouts, block_product(): picked = slots[:, columns]  146 us
    psum x2, blocking collectives, whole_orthonormal(): gram = lax.psum(jnp.dot(sketch, sketch.T, precision=HIGH), ('mesh', 'grp'))  130 us
    ppermute x28, starting transfers between devices, shifted(): return lax.ppermute(block, axis, route)  82.8 us
    dot_general x42, matrix products, block_product(): return jnp.einsum('sjq,qjr->sjr', picked, blocks, precision=HIGH)  77.7 us
    ppermute x28, waiting for transfers between devices, shifted(): return lax.ppermute(block, axis, route)  76.4 us
    reshape x42, local copies, waits for them, and re-layouts, block_product(): picked = picked.reshape(picked.shape[0], picked.shape[1], -1)  63.4 us
    ppermute x29, starting transfers between devices, extended_2(): lax.ppermute(tail, axis, [(i, (i + 1) % count) for i in range(ends)])  56.9 us
  transfers between devices with their start and end apart: 86, of which 21 were waited for; matrix products, arithmetic and copies ran while one was open for 17% of the time, Pallas kernels for 0%

commit v1 on v0

v1 whole, which is shorter than its diff:
```python
import functools
import math

import jax
import jax.numpy as jnp
from jax import lax
from jax.experimental import pallas as pl
from jax.experimental.pallas import tpu as pltpu
from jax.sharding import PartitionSpec as P

S = 32
BLOCK = 64
KL = 4
LEV = 8
RPL = 8
HB = 4
NB = 64
PAIR = 2 * BLOCK
QUAD = 4 * BLOCK
WIDE = RPL * BLOCK

LOWER_AT = 0
UPPER_AT = (LEV - 1) * RPL * KL
HALO_AT = 2 * UPPER_AT
PLAN_AT = HALO_AT + LEV * HB
PARITY_AT = PLAN_AT + NB

HIGH = lax.Precision.HIGHEST
AXES = ("mesh", "grp")
VMEM = pltpu.CompilerParams(vmem_limit_bytes=40 * 1024 * 1024)


def split(x):
    high = x.astype(jnp.bfloat16)
    low = (x - high.astype(jnp.float32)).astype(jnp.bfloat16)
    return high, low


def dot(a, b, dims=((1,), (0,))):
    return lax.dot_general(a, b, (dims, ((), ())), preferred_element_type=jnp.float32)


def dot3(a, b_high, b_low, dims=((1,), (0,))):
    a_high, a_low = split(a)
    return dot(a_high, b_high, dims) + (dot(a_low, b_high, dims) + dot(a_high, b_low, dims))


def first_half():
    return lax.broadcasted_iota(jnp.int32, (S, PAIR), 1) < BLOCK


def turned(tile):
    return pltpu.roll(tile, BLOCK, 1)


def doubled(tile):
    first = first_half()
    other = turned(tile)
    return jnp.where(first, tile, other), jnp.where(first, other, tile)


def parity_of(index):
    return jnp.bitwise_and(index, 1)


def pair_tile(ref, block):
    start = pl.multiple_of(lax.shift_right_logical(block, 1) * PAIR, PAIR)
    return pl.ds(start, PAIR)


def in_half(tile, block, half):
    return jnp.where(parity_of(block) == half, tile, turned(tile))


def listed(ints, level, ref):
    tiles = []
    first = first_half()
    for pair in range(HB // 2):
        h = [ints[HALO_AT + level * HB + 2 * pair + half] for half in range(2)]
        moved = [in_half(ref[:, pair_tile(ref, h[half])], h[half], half) for half in range(2)]
        tiles.append(jnp.where(first, moved[0], moved[1]))
    return jnp.concatenate(tiles, axis=1)


def own_blocks(out):
    first = first_half()
    rows = [out[j * S : (j + 1) * S] for j in range(4)]
    return jnp.concatenate(
        [
            jnp.where(first, rows[0][:, :PAIR], rows[1][:, :PAIR]),
            jnp.where(first, rows[2][:, PAIR:], rows[3][:, PAIR:]),
        ],
        axis=1,
    )


def spread(quad):
    lane = lax.shift_right_logical(lax.broadcasted_iota(jnp.int32, (S, QUAD), 1), 6)
    return jnp.concatenate([jnp.where(lane == j, quad, 0.0) for j in range(4)], axis=0)


def stacked(quad):
    parts = []
    for pair in range(2):
        tile = quad[:, pair * PAIR : (pair + 1) * PAIR]
        parts += [tile[:, :BLOCK], turned(tile)[:, :BLOCK]]
    return jnp.concatenate(parts, axis=0)


def send_listed_kernel(level, ints, field, send):
    send[...] = listed(ints, level, field)


def prepare_kernel(ints, forcing, inverse, y, send):
    for quad in range(NB // 4):
        rows = []
        for j in range(4):
            block = ints[PLAN_AT + 4 * quad + j]
            tile = forcing[:, pair_tile(forcing, block)]
            rows.append(in_half(tile, block, 0)[:, :BLOCK])
        lanes = slice(quad * QUAD, (quad + 1) * QUAD)
        inv_high, inv_low = split(inverse[:, lanes])
        y[:, lanes] = own_blocks(dot3(jnp.concatenate(rows, axis=0), inv_high, inv_low))
    send[...] = listed(ints, 0, y)


def compose_kernel(blocks, inverse, high, low):
    lane = lax.shift_right_logical(lax.broadcasted_iota(jnp.int32, (BLOCK, QUAD), 1), 6)
    for quad in range(2):
        lanes = slice(quad * QUAD, (quad + 1) * QUAD)
        inv = inverse[:, lanes]
        diagonal = jnp.concatenate([jnp.where(lane == j, inv, 0.0) for j in range(4)], axis=0)
        d_high, d_low = split(diagonal)
        product = dot3(blocks[:, lanes], d_high, d_low)
        p_high, p_low = split(product)
        high[:, lanes] = p_high
        low[:, lanes] = p_low


def combine_kernel(ints, x, y, w, diag, inverse, out):
    for quad in range(x.shape[1] // QUAD):
        lanes = slice(quad * QUAD, (quad + 1) * QUAD)
        d_high, d_low = split(diag[:, lanes])
        i_high, i_low = split(inverse[:, lanes])
        value = x[:, lanes]
        image = own_blocks(dot3(stacked(value), d_high, d_low))
        image = own_blocks(dot3(stacked(image), i_high, i_low))
        out[:, lanes] = 2.0 * value + y[:, lanes] - w[:, lanes] - image


def fill_slots(ints, slots, prev, swap0, swap1):
    for pair in range(RPL // 2):
        a, b = doubled(prev[:, pair * PAIR : (pair + 1) * PAIR])
        slots[2 * pair] = a
        slots[2 * pair + 1] = b
    odd = ints[PARITY_AT]
    for ref, base in ((swap1, RPL + HB * odd), (swap0, RPL + HB - HB * odd)):
        for pair in range(HB // 2):
            a, b = doubled(ref[:, pair * PAIR : (pair + 1) * PAIR])
            slots[base + 2 * pair] = a
            slots[base + 2 * pair + 1] = b


def gather_kernel(at, level, send_on, ints, base, high, low, prev, swap0, swap1, out, *rest):
    slots = rest[-1]
    fill_slots(ints, slots, prev, swap0, swap1)
    first = first_half()
    for quad in range(2):
        rows = []
        for j in range(4):
            c = [ints[at + (quad * 4 + j) * KL + k] for k in range(KL)]
            rows.append(
                jnp.concatenate(
                    [
                        jnp.where(first, slots[c[0]], slots[c[1]]),
                        jnp.where(first, slots[c[2]], slots[c[3]]),
                    ],
                    axis=1,
                )
            )
        lanes = slice(quad * QUAD, (quad + 1) * QUAD)
        product = dot3(jnp.concatenate(rows, axis=0), high[:, lanes], low[:, lanes])
        out[:, lanes] = base[:, lanes] - own_blocks(product)
    if send_on:
        rest[0][...] = listed(ints, level, out)


def add_listed(ints, level, out, arriving):
    first = first_half()
    for i in range(HB):
        h = ints[HALO_AT + level * HB + i]
        tile = arriving[:, (i // 2) * PAIR : (i // 2 + 1) * PAIR]
        tile = jnp.where(parity_of(h) == i % 2, tile, turned(tile))
        keep = first == (parity_of(h) == 0)
        lanes = pair_tile(out, h)
        out[:, lanes] = out[:, lanes] - jnp.where(keep, tile, 0.0)


def push_kernel(at, level, first_level, last_level, ints, *refs):
    refs = list(refs)
    source = refs.pop(0)
    if not first_level:
        own_in, swap0, swap1 = refs.pop(0), refs.pop(0), refs.pop(0)
    if not last_level:
        high, low = refs.pop(0), refs.pop(0)
    if not first_level:
        out = refs.pop(0)
        out[...] = source[...] - own_in[...]
        add_listed(ints, level, out, swap0[...] + swap1[...])
    else:
        out = source
    if last_level:
        return
    own, send0, send1, slots = refs
    slots[...] = jnp.zeros_like(slots)
    first = first_half()
    for quad in range(2):
        lanes = slice(quad * QUAD, (quad + 1) * QUAD)
        terms = dot3(spread(out[:, lanes]), high[:, lanes], low[:, lanes], ((1,), (1,)))
        for j in range(4):
            for k in range(KL):
                c = ints[at + (quad * 4 + j) * KL + k]
                tile = terms[j * S : (j + 1) * S, (k // 2) * PAIR : (k // 2 + 1) * PAIR]
                keep = first if k % 2 == 0 else jnp.logical_not(first)
                slots[c] += jnp.where(keep, tile, 0.0)

    def total(c):
        value = slots[c]
        return value + turned(value)

    for pair in range(RPL // 2):
        own[:, pair * PAIR : (pair + 1) * PAIR] = jnp.where(
            first, total(2 * pair), total(2 * pair + 1)
        )
    odd = ints[PARITY_AT]
    for ref, base in ((send1, RPL + HB * odd), (send0, RPL + HB - HB * odd)):
        for pair in range(HB // 2):
            ref[:, pair * PAIR : (pair + 1) * PAIR] = jnp.where(
                first, total(base + 2 * pair), total(base + 2 * pair + 1)
            )


def finish_kernel(ints, turn, field, inverse, out, natural):
    first = first_half()
    for quad in range(NB // 4):
        lanes = slice(quad * QUAD, (quad + 1) * QUAD)
        i_high, i_low = split(inverse[:, lanes])
        product = dot3(spread(field[:, lanes]), i_high, i_low, ((1,), (1,)))
        for j in range(4):
            block = ints[PLAN_AT + 4 * quad + j]
            piece = product[j * S : (j + 1) * S]
            piece = jnp.concatenate([piece, piece], axis=1)
            place(natural, block, piece, first)
    out[...] = lax.dot_general(
        turn[...], natural[...], (((1,), (0,)), ((), ())), precision=HIGH, preferred_element_type=jnp.float32
    )


def place(natural, block, piece, first):
    keep = first == (parity_of(block) == 0)
    lanes = pair_tile(natural, block)
    natural[:, lanes] = jnp.where(keep, piece, natural[:, lanes])


def basis_kernel(ints, turn, field, out, natural):
    first = first_half()
    for pair in range(NB // 2):
        a, b = doubled(field[:, pair * PAIR : (pair + 1) * PAIR])
        place(natural, ints[PLAN_AT + 2 * pair], a, first)
        place(natural, ints[PLAN_AT + 2 * pair + 1], b, first)
    out[...] = lax.dot_general(
        turn[...], natural[...], (((1,), (0,)), ((), ())), precision=HIGH, preferred_element_type=jnp.float32
    )


SMEM_SPEC = pl.BlockSpec(memory_space=pltpu.SMEM)
VMEM_SPEC = pl.BlockSpec(memory_space=pltpu.VMEM)


def call(kernel, operands, outs, scratch=(), flops=0, smem=True):
    in_specs = [VMEM_SPEC] * len(operands)
    if smem:
        in_specs[0] = SMEM_SPEC
    moved = 4 * sum(math.prod(o.shape) for o in operands) + 4 * sum(math.prod(o) for o, _ in outs)
    return pl.pallas_call(
        kernel,
        out_shape=[jax.ShapeDtypeStruct(shape, dtype) for shape, dtype in outs],
        in_specs=in_specs,
        out_specs=[VMEM_SPEC] * len(outs),
        scratch_shapes=list(scratch),
        compiler_params=VMEM,
        cost_estimate=pl.CostEstimate(flops=flops, bytes_accessed=moved, transcendentals=0),
    )(*operands)


F32 = jnp.float32
BF16 = jnp.bfloat16
LEVEL_FIELD = ((S, WIDE), F32)
SENT = ((S, HB * BLOCK), F32)
SLOTS = pltpu.VMEM((RPL + 2 * HB, S, PAIR), F32)


def swap(sent0, sent1):
    count = lax.axis_size(AXES)
    even = [(i, i ^ 1) for i in range(count)]
    other = [((i + 1) ^ 1) - 1 for i in range(count)]
    odd = [(i, j) for i, j in enumerate(other) if 0 <= j < count]
    swap1 = lax.ppermute(sent1, AXES, odd)
    swap0 = lax.ppermute(sent0, AXES, even)
    return swap0, swap1


def shards(forcing, plan, lower_blocks, lower_columns, upper_blocks, upper_columns, diag_blocks, inverse_blocks, halo_list):
    parity = lax.rem(lax.axis_index(AXES), 2).astype(jnp.int32)
    ints = jnp.concatenate(
        [
            lower_columns.reshape(-1),
            upper_columns.reshape(-1),
            halo_list.reshape(-1),
            plan.reshape(-1),
            parity.reshape(1),
        ]
    )

    def level_of(array, level):
        return array[:, level * WIDE : (level + 1) * WIDE]

    y, sent = call(prepare_kernel, [ints, forcing, inverse_blocks], [((S, NB * BLOCK), F32), SENT])
    lower = []
    upper = []
    wide = ((KL * BLOCK, WIDE), BF16)
    for level in range(LEV - 1):
        lower.append(
            call(
                compose_kernel,
                [level_of(lower_blocks, level), level_of(inverse_blocks, level + 1)],
                [wide, wide],
                flops=2 * 6 * 256**3,
                smem=False,
            )
        )
    for level in range(LEV - 1):
        upper.append(
            call(
                compose_kernel,
                [level_of(upper_blocks, level), level_of(inverse_blocks, level)],
                [wide, wide],
                flops=2 * 6 * 256**3,
                smem=False,
            )
        )

    def gather(base, blocks, at, level, prev, sent, send_on):
        swap0, swap1 = swap(sent, sent)
        outs = call(
            functools.partial(gather_kernel, at, level, send_on),
            [ints, base, *blocks, prev, swap0, swap1],
            [LEVEL_FIELD, SENT] if send_on else [LEVEL_FIELD],
            [SLOTS],
        )
        return (outs[0], outs[1]) if send_on else (outs[0], None)

    def ascend(base, sent):
        field = [base[0]]
        for level in range(1, LEV):
            value, sent = gather(
                base[level], lower[level - 1], LOWER_AT + (level - 1) * RPL * KL, level, field[-1], sent, True
            )
            field.append(value)
        return field, sent

    def descend(base, sent):
        field = [None] * LEV
        field[LEV - 1] = base[LEV - 1]
        for level in range(LEV - 2, -1, -1):
            field[level], sent = gather(
                base[level], upper[level], UPPER_AT + level * RPL * KL, level, field[level + 1], sent, level > 0
            )
        return field

    y = [level_of(y, level) for level in range(LEV)]
    w, sent = ascend(y, sent)
    x = descend(w, sent)

    def combine(levels):
        join = lambda field: jnp.concatenate([field[level] for level in levels], axis=1) if len(levels) > 1 else field[levels[0]]
        part = slice(levels[0] * WIDE, (levels[-1] + 1) * WIDE)
        out = call(
            combine_kernel,
            [ints, join(x), join(y), join(w), diag_blocks[:, part], inverse_blocks[:, part]],
            [((S, WIDE * len(levels)), F32)],
        )[0]
        return [out[:, i * WIDE : (i + 1) * WIDE] for i in range(len(levels))]

    c = combine([0])
    sent = call(functools.partial(send_listed_kernel, 0), [ints, c[0]], [SENT])[0]
    for level in range(1, LEV):
        c += combine([level])
    v, sent = ascend(c, sent)
    sketch = descend([v[level] + w[level] - x[level] for level in range(LEV)], sent)

    def push(source, level, own, swaps, blocks, at):
        outs = [] if own is None else [LEVEL_FIELD]
        operands = [ints, source] + ([] if own is None else [own, *swaps])
        if blocks is not None:
            operands += blocks
            outs = outs + [LEVEL_FIELD, SENT, SENT]
        results = list(
            call(
                functools.partial(push_kernel, at, level, own is None, blocks is None),
                operands,
                outs,
                [SLOTS] if blocks is not None else [],
            )
        )
        value = source if own is None else results.pop(0)
        if blocks is None:
            return value, None, None
        return value, results[0], swap(results[1], results[2])

    before = [None] * LEV
    own = swaps = None
    for level in range(LEV - 1):
        before[level], own, swaps = push(sketch[level], level, own, swaps, upper[level], UPPER_AT + level * RPL * KL)
    last = LEV - 1
    turned_back = [None] * LEV
    before[last], _, _ = push(sketch[last], last, own, swaps, None, 0)
    own = swaps = None
    for level in range(LEV - 1, 0, -1):
        turned_back[level], own, swaps = push(
            before[level], level, own, swaps, lower[level - 1], LOWER_AT + (level - 1) * RPL * KL
        )
    turned_back[0], _, _ = push(before[0], 0, own, swaps, None, 0)

    columns = jnp.concatenate(sketch, axis=1)
    gram = lax.psum(jnp.dot(columns, columns.T, precision=HIGH), AXES)
    unit = jnp.eye(S, dtype=F32)
    first = jax.scipy.linalg.solve_triangular(jnp.linalg.cholesky(gram), unit, lower=True)
    ortho = jnp.dot(first, columns, precision=HIGH)
    gram = lax.psum(jnp.dot(ortho, ortho.T, precision=HIGH), AXES)
    second = jax.scipy.linalg.solve_triangular(jnp.linalg.cholesky(gram), unit, lower=True)
    second = second * math.sqrt(NB * BLOCK * lax.axis_size(AXES))
    both = jnp.dot(second, first, precision=HIGH)
    natural = [((S, NB * BLOCK), F32)]
    room = [pltpu.VMEM((S, NB * BLOCK), F32)]
    basis = call(basis_kernel, [ints, second, ortho], natural, room)[0]
    field = jnp.concatenate(turned_back, axis=1)
    adjoint_field = call(finish_kernel, [ints, both, field, inverse_blocks], natural, room)[0]
    return (basis, adjoint_field)


def solution(mesh):
    in_specs = (
        P(None, AXES),
        P(AXES, None),
        P(None, AXES),
        P(AXES, None),
        P(None, AXES),
        P(AXES, None),
        P(None, AXES),
        P(None, AXES),
        P(AXES, None),
    )
    out_specs = (P(None, AXES), P(None, AXES))
    return jax.shard_map(shards, mesh=mesh, in_specs=in_specs, out_specs=out_specs, check_vma=False)
```

time: 1360 us -> 648 us (0.48); the launches traced: 1330 us -> 636 us
  local copies, waits for them, and re-layouts: 467 us -> 51.7 us
  matrix products: 161 us -> 7.18 us
  starting transfers between devices: 368 us -> 229 us
  other arithmetic: 116 us -> 23.6 us
  Pallas kernels: 0 us -> 73.6 us
  waiting for transfers between devices: 86.2 us -> 121 us
    reshape x279 -> x3, local copies, waits for them, and re-layouts: 196 us -> 0.28 us  [the longest x1 0.1 us: shards(): upper_columns.reshape(-1)]
    gather x144 -> x0, local copies, waits for them, and re-layouts: 194 us -> none  [the longest x84 146 us: block_product(): picked = slots[:, columns]]
    dot_general x111 -> x4, matrix products: 159 us -> 6.05 us  [the longest x1 2.43 us: shards(): gram = lax.psum(jnp.dot(columns, columns.T, precision=HIGH), AXES)]
    ppermute x86 -> x84, starting transfers between devices: 368 us -> 229 us  [the longest x42 225 us: swap(): swap1 = lax.ppermute(sent1, AXES, odd)]
    pallas_call x0 -> x70, Pallas kernels: none -> 73.6 us  [call(): pl.pallas_call(kernel, out_shape=[jax.ShapeDtypeStruct(shape, dtype) for...]
    scatter-add x28 -> x0, other arithmetic: 56.2 us -> none  [the longest x14 37.9 us: push_terms(): jnp.zeros((values.shape[0], RPL + 2 * HB, BLOCK), jnp.float32)]
    ppermute x86 -> x84, waiting for transfers between devices: 86.2 us -> 121 us  [the longest x42 118 us: swap(): swap1 = lax.ppermute(sent1, AXES, odd)]
    unnamed x232 -> x191, local copies, waits for them, and re-layouts: 19.7 us -> 46.1 us
  transfers between devices with their start and end apart: 86 -> 84, of which waited for: 21 -> 40; matrix products, arithmetic and copies ran while one was open for 17% -> 6% of each run, Pallas kernels for 0% -> 3%
where the time goes in v1:
time: 648 us; the launch traced here: 636 us
  starting transfers between devices  229 us (35%)
  blocking collectives  127 us (20%)
  waiting for transfers between devices  121 us (19%)
  Pallas kernels  73.6 us (11%)
  local copies, waits for them, and re-layouts  51.7 us (8%)
  other arithmetic  23.6 us (4%)
  matrix products  7.18 us (1%)
    ppermute x42, starting transfers between devices, swap(): swap1 = lax.ppermute(sent1, AXES, odd)  225 us
    ppermute x42, waiting for transfers between devices, swap(): swap1 = lax.ppermute(sent1, AXES, odd)  118 us
    pallas_call x70, Pallas kernels, call(): pl.pallas_call(kernel, out_shape=[jax.ShapeDtypeStruct(shape, dtype) for...  73.6 us
    psum x1, blocking collectives, shards(): gram = lax.psum(jnp.dot(columns, columns.T, precision=HIGH), AXES)  63.5 us
    psum x1, blocking collectives, shards(): gram = lax.psum(jnp.dot(ortho, ortho.T, precision=HIGH), AXES)  63.1 us
    unnamed x191, local copies, waits for them, and re-layouts  46.1 us
  transfers between devices with their start and end apart: 84, of which 40 were waited for; matrix products, arithmetic and copies ran while one was open for 6% of the time, Pallas kernels for 3%

profile of v1, /device:TPU:2, one launch (start us, length us, event | category | flops | bytes accessed | tf_op | source)
XLA Modules:
  0.0 635.8 jit_solution(11808712160319747735)
XLA Ops:
  7.9 7.8 %collective-permute-start.1 = (f32[32,256]{1,0:T(8,128)S(1)}, f32[32,256]{1,0:T(8,128)S(1)}, u32[]{:S(2)}, u32[]{:S(2)}) collective-permute-start(f32[32,256]{1,0:T(8,128)S(1)} %get-tuple-element.145), channel_id=1, source_target_pairs={{1,2},{2,1},{3,4},{4,3},{5,6},{6,5},{7,8},{8,7},{9,10},{10,9},{11,... | collective-permute-start | bytes 98312 | tf_op jit(solution)/shard_map/ppermute | solution.py:308
  20.8 5.5 collective-permute-start.3
  26.7 3.5 collective-permute-done.3.swap1
  31.2 5.5 collective-permute-start.5
  41.7 5.5 collective-permute-start.7
  47.7 3.5 collective-permute-done.7.swap1
  52.2 5.5 collective-permute-start.9
  62.7 5.5 collective-permute-start.11
  73.1 5.5 collective-permute-start.13
  83.6 5.5 collective-permute-start.15
  94.1 5.4 collective-permute-start.17
  104.6 5.5 collective-permute-start.19
  115.0 5.5 collective-permute-start.21
  125.5 5.5 collective-permute-start.23
  136.2 5.3 collective-permute-start.25
  142.0 3.6 collective-permute-done.25.swap1
  146.6 5.3 collective-permute-start.27
  152.5 3.6 collective-permute-done.27.swap1
  158.9 5.4 collective-permute-start.29
  169.4 5.4 collective-permute-start.31
  179.9 5.4 collective-permute-start.33
  190.3 5.5 collective-permute-start.35
  200.9 5.5 collective-permute-start.37
  211.3 5.5 collective-permute-start.39
  221.8 5.5 collective-permute-start.41
  232.3 5.5 collective-permute-start.43
  237.9 3.9 collective-permute-done.43.swap1
  242.8 5.5 collective-permute-start.45
  248.4 3.9 collective-permute-done.45.swap1
  253.3 5.5 collective-permute-start.47
  258.9 3.9 collective-permute-done.47.swap1
  263.8 5.5 collective-permute-start.49
  269.4 3.9 collective-permute-done.49.swap1
  274.3 5.5 collective-permute-start.51
  279.9 3.9 collective-permute-done.51.swap1
  284.8 5.6 collective-permute-start.53
  290.5 3.9 collective-permute-done.53.swap1
  295.5 5.4 collective-permute-start.55
  301.0 3.9 collective-permute-done.55.swap1
  308.3 5.4 collective-permute-start.57
  320.7 63.5 %psum.14 = f32[32,32]{0,1:T(8,128)} all-reduce(f32[32,32]{0,1:T(8,128)} %fusion.16), channel_id=1, replica_groups=mesh['mesh'=32,'grp'=4] {'mesh','grp'}, use_global_device_ids=true, to_apply=%region_0.0 | all-reduce | flops 1024 | bytes 8192 | tf_op jit(solution)/shard_map/psum | solution.py:436
  392.5 4.8 collective-permute-start.59
  398.6 4.2 cholesky.44
  408.5 5.0 collective-permute-start.61
  414.2 3.7 collective-permute-done.61.refs_3_
  422.5 5.0 collective-permute-start.63
  428.2 3.7 collective-permute-done.63.refs_3_
  437.8 5.0 collective-permute-start.65
  444.7 3.8 custom-call.6
  452.3 4.8 collective-permute-start.67
  458.0 3.7 collective-permute-done.67.refs_3_
  463.9 4.8 collective-permute-start.69
  475.8 4.8 collective-permute-start.71
  481.7 63.1 %psum.15 = f32[32,32]{0,1:T(8,128)} all-reduce(f32[32,32]{0,1:T(8,128)} %fusion.18), channel_id=1, replica_groups=mesh['mesh'=32,'grp'=4] {'mesh','grp'}, use_global_device_ids=true, to_apply=%region_3.6 | all-reduce | flops 1024 | bytes 8192 | tf_op jit(solution)/shard_map/psum | solution.py:440
  553.5 4.5 collective-permute-start.73
  559.3 4.2 cholesky.55
  571.8 5.2 collective-permute-start.75
  577.8 3.5 collective-permute-done.75.refs_3_
  584.9 5.3 collective-permute-start.77
  590.9 3.6 collective-permute-done.77.refs_3_
  597.8 5.2 collective-permute-start.79
  610.5 5.2 collective-permute-start.81
  615.9 4.0 collective-permute-done.81.refs_3_
  622.1 5.2 collective-permute-start.83
  (405 shorter events, 205.6 us)
Async XLA Ops:
  7.9 9.5 %collective-permute-start.1 = (f32[32,256]{1,0:T(8,128)S(1)}, f32[32,256]{1,0:T(8,128)S(1)}, u32[]{:S(2)}, u32[]{:S(2)}) collective-permute-start(f32[32,256]{1,0:T(8,128)S(1)} %get-tuple-element.145), channel_id=1, source_target_pairs={{1,2},{2,1},{3,4},{4,3},{5,6},{6,5},{7,8},{8,7},{9,10},{10,9},{11,... | collective-permute-start | bytes 98312 | tf_op jit(solution)/shard_map/ppermute | solution.py:308
  20.8 9.5 %collective-permute-start.3 = (f32[32,256]{1,0:T(8,128)S(1)}, f32[32,256]{1,0:T(8,128)S(1)}, u32[]{:S(2)}, u32[]{:S(2)}) collective-permute-start(f32[32,256]{1,0:T(8,128)S(1)} %get-tuple-element.151), channel_id=1, source_target_pairs={{1,2},{2,1},{3,4},{4,3},{5,6},{6,5},{7,8},{8,7},{9,10},{10,9},{11,... | collective-permute-start | bytes 98312 | tf_op jit(solution)/shard_map/ppermute | solution.py:308
  31.2 9.5 %collective-permute-start.5 = (f32[32,256]{1,0:T(8,128)S(1)}, f32[32,256]{1,0:T(8,128)S(1)}, u32[]{:S(2)}, u32[]{:S(2)}) collective-permute-start(f32[32,256]{1,0:T(8,128)S(1)} %get-tuple-element.157), channel_id=1, source_target_pairs={{1,2},{2,1},{3,4},{4,3},{5,6},{6,5},{7,8},{8,7},{9,10},{10,9},{11,... | collective-permute-start | bytes 98312 | tf_op jit(solution)/shard_map/ppermute | solution.py:308
  41.7 9.5 %collective-permute-start.7 = (f32[32,256]{1,0:T(8,128)S(1)}, f32[32,256]{1,0:T(8,128)S(1)}, u32[]{:S(2)}, u32[]{:S(2)}) collective-permute-start(f32[32,256]{1,0:T(8,128)S(1)} %get-tuple-element.163), channel_id=1, source_target_pairs={{1,2},{2,1},{3,4},{4,3},{5,6},{6,5},{7,8},{8,7},{9,10},{10,9},{11,... | collective-permute-start | bytes 98312 | tf_op jit(solution)/shard_map/ppermute | solution.py:308
  52.2 9.5 %collective-permute-start.9 = (f32[32,256]{1,0:T(8,128)S(1)}, f32[32,256]{1,0:T(8,128)S(1)}, u32[]{:S(2)}, u32[]{:S(2)}) collective-permute-start(f32[32,256]{1,0:T(8,128)S(1)} %get-tuple-element.169), channel_id=1, source_target_pairs={{1,2},{2,1},{3,4},{4,3},{5,6},{6,5},{7,8},{8,7},{9,10},{10,9},{11,... | collective-permute-start | bytes 98312 | tf_op jit(solution)/shard_map/ppermute | solution.py:308
  62.7 9.5 %collective-permute-start.11 = (f32[32,256]{1,0:T(8,128)S(1)}, f32[32,256]{1,0:T(8,128)S(1)}, u32[]{:S(2)}, u32[]{:S(2)}) collective-permute-start(f32[32,256]{1,0:T(8,128)S(1)} %get-tuple-element.175), channel_id=1, source_target_pairs={{1,2},{2,1},{3,4},{4,3},{5,6},{6,5},{7,8},{8,7},{9,10},{10,9},{11,... | collective-permute-start | bytes 98312 | tf_op jit(solution)/shard_map/ppermute | solution.py:308
  73.1 9.5 %collective-permute-start.13 = (f32[32,256]{1,0:T(8,128)S(1)}, f32[32,256]{1,0:T(8,128)S(1)}, u32[]{:S(2)}, u32[]{:S(2)}) collective-permute-start(f32[32,256]{1,0:T(8,128)S(1)} %get-tuple-element.181), channel_id=1, source_target_pairs={{1,2},{2,1},{3,4},{4,3},{5,6},{6,5},{7,8},{8,7},{9,10},{10,9},{11,... | collective-permute-start | bytes 98312 | tf_op jit(solution)/shard_map/ppermute | solution.py:308
  83.6 9.5 %collective-permute-start.15 = (f32[32,256]{1,0:T(8,128)S(1)}, f32[32,256]{1,0:T(8,128)S(1)}, u32[]{:S(2)}, u32[]{:S(2)}) collective-permute-start(f32[32,256]{1,0:T(8,128)S(1)} %get-tuple-element.183), channel_id=1, source_target_pairs={{1,2},{2,1},{3,4},{4,3},{5,6},{6,5},{7,8},{8,7},{9,10},{10,9},{11,... | collective-permute-start | bytes 98312 | tf_op jit(solution)/shard_map/ppermute | solution.py:308
  94.1 9.5 %collective-permute-start.17 = (f32[32,256]{1,0:T(8,128)S(1)}, f32[32,256]{1,0:T(8,128)S(1)}, u32[]{:S(2)}, u32[]{:S(2)}) collective-permute-start(f32[32,256]{1,0:T(8,128)S(1)} %get-tuple-element.185), channel_id=1, source_target_pairs={{1,2},{2,1},{3,4},{4,3},{5,6},{6,5},{7,8},{8,7},{9,10},{10,9},{11,... | collective-permute-start | bytes 98312 | tf_op jit(solution)/shard_map/ppermute | solution.py:308
  99.5 4.0 collective-permute-start.16
  104.6 9.5 %collective-permute-start.19 = (f32[32,256]{1,0:T(8,128)S(1)}, f32[32,256]{1,0:T(8,128)S(1)}, u32[]{:S(2)}, u32[]{:S(2)}) collective-permute-start(f32[32,256]{1,0:T(8,128)S(1)} %get-tuple-element.187), channel_id=1, source_target_pairs={{1,2},{2,1},{3,4},{4,3},{5,6},{6,5},{7,8},{8,7},{9,10},{10,9},{11,... | collective-permute-start | bytes 98312 | tf_op jit(solution)/shard_map/ppermute | solution.py:308
  115.0 9.5 %collective-permute-start.21 = (f32[32,256]{1,0:T(8,128)S(1)}, f32[32,256]{1,0:T(8,128)S(1)}, u32[]{:S(2)}, u32[]{:S(2)}) collective-permute-start(f32[32,256]{1,0:T(8,128)S(1)} %get-tuple-element.189), channel_id=1, source_target_pairs={{1,2},{2,1},{3,4},{4,3},{5,6},{6,5},{7,8},{8,7},{9,10},{10,9},{11,... | collective-permute-start | bytes 98312 | tf_op jit(solution)/shard_map/ppermute | solution.py:308
  125.5 9.5 %collective-permute-start.23 = (f32[32,256]{1,0:T(8,128)S(1)}, f32[32,256]{1,0:T(8,128)S(1)}, u32[]{:S(2)}, u32[]{:S(2)}) collective-permute-start(f32[32,256]{1,0:T(8,128)S(1)} %get-tuple-element.191), channel_id=1, source_target_pairs={{1,2},{2,1},{3,4},{4,3},{5,6},{6,5},{7,8},{8,7},{9,10},{10,9},{11,... | collective-permute-start | bytes 98312 | tf_op jit(solution)/shard_map/ppermute | solution.py:308
  131.0 4.2 collective-permute-start.22
  136.2 9.5 %collective-permute-start.25 = (f32[32,256]{1,0:T(8,128)S(1)}, f32[32,256]{1,0:T(8,128)S(1)}, u32[]{:S(2)}, u32[]{:S(2)}) collective-permute-start(f32[32,256]{1,0:T(8,128)S(1)} %get-tuple-element.193), channel_id=1, source_target_pairs={{1,2},{2,1},{3,4},{4,3},{5,6},{6,5},{7,8},{8,7},{9,10},{10,9},{11,... | collective-permute-start | bytes 98312 | tf_op jit(solution)/shard_map/ppermute | solution.py:308
  141.5 4.2 collective-permute-start.24
  146.6 9.5 %collective-permute-start.27 = (f32[32,256]{1,0:T(8,128)S(1)}, f32[32,256]{1,0:T(8,128)S(1)}, u32[]{:S(2)}, u32[]{:S(2)}) collective-permute-start(f32[32,256]{1,0:T(8,128)S(1)} %get-tuple-element.195), channel_id=1, source_target_pairs={{1,2},{2,1},{3,4},{4,3},{5,6},{6,5},{7,8},{8,7},{9,10},{10,9},{11,... | collective-permute-start | bytes 98312 | tf_op jit(solution)/shard_map/ppermute | solution.py:308
  151.9 4.2 collective-permute-start.26
  158.9 9.5 %collective-permute-start.29 = (f32[32,256]{1,0:T(8,128)S(1)}, f32[32,256]{1,0:T(8,128)S(1)}, u32[]{:S(2)}, u32[]{:S(2)}) collective-permute-start(f32[32,256]{1,0:T(8,128)S(1)} %shard_map.135), channel_id=1, source_target_pairs={{1,2},{2,1},{3,4},{4,3},{5,6},{6,5},{7,8},{8,7},{9,10},{10,9},{11,... | collective-permute-start | bytes 98312 | tf_op jit(solution)/shard_map/ppermute | solution.py:308
  164.3 4.0 collective-permute-start.28
  169.4 9.5 %collective-permute-start.31 = (f32[32,256]{1,0:T(8,128)S(1)}, f32[32,256]{1,0:T(8,128)S(1)}, u32[]{:S(2)}, u32[]{:S(2)}) collective-permute-start(f32[32,256]{1,0:T(8,128)S(1)} %get-tuple-element.197), channel_id=1, source_target_pairs={{1,2},{2,1},{3,4},{4,3},{5,6},{6,5},{7,8},{8,7},{9,10},{10,9},{11,... | collective-permute-start | bytes 98312 | tf_op jit(solution)/shard_map/ppermute | solution.py:308
  174.8 4.1 collective-permute-start.30
  179.9 9.5 %collective-permute-start.33 = (f32[32,256]{1,0:T(8,128)S(1)}, f32[32,256]{1,0:T(8,128)S(1)}, u32[]{:S(2)}, u32[]{:S(2)}) collective-permute-start(f32[32,256]{1,0:T(8,128)S(1)} %get-tuple-element.199), channel_id=1, source_target_pairs={{1,2},{2,1},{3,4},{4,3},{5,6},{6,5},{7,8},{8,7},{9,10},{10,9},{11,... | collective-permute-start | bytes 98312 | tf_op jit(solution)/shard_map/ppermute | solution.py:308
  185.3 4.1 collective-permute-start.32
  190.3 9.5 %collective-permute-start.35 = (f32[32,256]{1,0:T(8,128)S(1)}, f32[32,256]{1,0:T(8,128)S(1)}, u32[]{:S(2)}, u32[]{:S(2)}) collective-permute-start(f32[32,256]{1,0:T(8,128)S(1)} %get-tuple-element.201), channel_id=1, source_target_pairs={{1,2},{2,1},{3,4},{4,3},{5,6},{6,5},{7,8},{8,7},{9,10},{10,9},{11,... | collective-permute-start | bytes 98312 | tf_op jit(solution)/shard_map/ppermute | solution.py:308
  200.9 9.5 %collective-permute-start.37 = (f32[32,256]{1,0:T(8,128)S(1)}, f32[32,256]{1,0:T(8,128)S(1)}, u32[]{:S(2)}, u32[]{:S(2)}) collective-permute-start(f32[32,256]{1,0:T(8,128)S(1)} %get-tuple-element.203), channel_id=1, source_target_pairs={{1,2},{2,1},{3,4},{4,3},{5,6},{6,5},{7,8},{8,7},{9,10},{10,9},{11,... | collective-permute-start | bytes 98312 | tf_op jit(solution)/shard_map/ppermute | solution.py:308
  211.3 9.5 %collective-permute-start.39 = (f32[32,256]{1,0:T(8,128)S(1)}, f32[32,256]{1,0:T(8,128)S(1)}, u32[]{:S(2)}, u32[]{:S(2)}) collective-permute-start(f32[32,256]{1,0:T(8,128)S(1)} %get-tuple-element.205), channel_id=1, source_target_pairs={{1,2},{2,1},{3,4},{4,3},{5,6},{6,5},{7,8},{8,7},{9,10},{10,9},{11,... | collective-permute-start | bytes 98312 | tf_op jit(solution)/shard_map/ppermute | solution.py:308
  221.8 9.5 %collective-permute-start.41 = (f32[32,256]{1,0:T(8,128)S(1)}, f32[32,256]{1,0:T(8,128)S(1)}, u32[]{:S(2)}, u32[]{:S(2)}) collective-permute-start(f32[32,256]{1,0:T(8,128)S(1)} %get-tuple-element.207), channel_id=1, source_target_pairs={{1,2},{2,1},{3,4},{4,3},{5,6},{6,5},{7,8},{8,7},{9,10},{10,9},{11,... | collective-permute-start | bytes 98312 | tf_op jit(solution)/shard_map/ppermute | solution.py:308
  232.3 9.5 %collective-permute-start.43 = (f32[32,256]{1,0:T(8,128)S(1)}, f32[32,256]{1,0:T(8,128)S(1)}, u32[]{:S(2)}, u32[]{:S(2)}) collective-permute-start(f32[32,256]{1,0:T(8,128)S(1)} %get-tuple-element.209), channel_id=1, source_target_pairs={{1,2},{2,1},{3,4},{4,3},{5,6},{6,5},{7,8},{8,7},{9,10},{10,9},{11,... | collective-permute-start | bytes 98312 | tf_op jit(solution)/shard_map/ppermute | solution.py:308
  242.8 9.5 %collective-permute-start.45 = (f32[32,256]{1,0:T(8,128)S(1)}, f32[32,256]{1,0:T(8,128)S(1)}, u32[]{:S(2)}, u32[]{:S(2)}) collective-permute-start(f32[32,256]{1,0:T(8,128)S(1)} %get-tuple-element.211), channel_id=1, source_target_pairs={{1,2},{2,1},{3,4},{4,3},{5,6},{6,5},{7,8},{8,7},{9,10},{10,9},{11,... | collective-permute-start | bytes 98312 | tf_op jit(solution)/shard_map/ppermute | solution.py:308
  253.3 9.5 %collective-permute-start.47 = (f32[32,256]{1,0:T(8,128)S(1)}, f32[32,256]{1,0:T(8,128)S(1)}, u32[]{:S(2)}, u32[]{:S(2)}) collective-permute-start(f32[32,256]{1,0:T(8,128)S(1)} %get-tuple-element.213), channel_id=1, source_target_pairs={{1,2},{2,1},{3,4},{4,3},{5,6},{6,5},{7,8},{8,7},{9,10},{10,9},{11,... | collective-permute-start | bytes 98312 | tf_op jit(solution)/shard_map/ppermute | solution.py:308
  263.8 9.5 %collective-permute-start.49 = (f32[32,256]{1,0:T(8,128)S(1)}, f32[32,256]{1,0:T(8,128)S(1)}, u32[]{:S(2)}, u32[]{:S(2)}) collective-permute-start(f32[32,256]{1,0:T(8,128)S(1)} %get-tuple-element.215), channel_id=1, source_target_pairs={{1,2},{2,1},{3,4},{4,3},{5,6},{6,5},{7,8},{8,7},{9,10},{10,9},{11,... | collective-permute-start | bytes 98312 | tf_op jit(solution)/shard_map/ppermute | solution.py:308
  274.3 9.5 %collective-permute-start.51 = (f32[32,256]{1,0:T(8,128)S(1)}, f32[32,256]{1,0:T(8,128)S(1)}, u32[]{:S(2)}, u32[]{:S(2)}) collective-permute-start(f32[32,256]{1,0:T(8,128)S(1)} %get-tuple-element.217), channel_id=1, source_target_pairs={{1,2},{2,1},{3,4},{4,3},{5,6},{6,5},{7,8},{8,7},{9,10},{10,9},{11,... | collective-permute-start | bytes 98312 | tf_op jit(solution)/shard_map/ppermute | solution.py:308
  284.8 9.6 %collective-permute-start.53 = (f32[32,256]{1,0:T(8,128)S(1)}, f32[32,256]{1,0:T(8,128)S(1)}, u32[]{:S(2)}, u32[]{:S(2)}) collective-permute-start(f32[32,256]{1,0:T(8,128)S(1)} %get-tuple-element.219), channel_id=1, source_target_pairs={{1,2},{2,1},{3,4},{4,3},{5,6},{6,5},{7,8},{8,7},{9,10},{10,9},{11,... | collective-permute-start | bytes 98312 | tf_op jit(solution)/shard_map/ppermute | solution.py:308
  295.5 9.5 %collective-permute-start.55 = (f32[32,256]{1,0:T(8,128)S(1)}, f32[32,256]{1,0:T(8,128)S(1)}, u32[]{:S(2)}, u32[]{:S(2)}) collective-permute-start(f32[32,256]{1,0:T(8,128)S(1)} %get-tuple-element.221), channel_id=1, source_target_pairs={{1,2},{2,1},{3,4},{4,3},{5,6},{6,5},{7,8},{8,7},{9,10},{10,9},{11,... | collective-permute-start | bytes 98312 | tf_op jit(solution)/shard_map/ppermute | solution.py:308
  300.9 4.0 collective-permute-start.54
  308.3 77.3 %collective-permute-start.56 = (f32[32,256]{1,0:T(8,128)}, f32[32,256]{1,0:T(8,128)}, u32[]{:S(2)}, u32[]{:S(2)}) collective-permute-start(f32[32,256]{1,0:T(8,128)} %get-tuple-element.223), channel_id=1, source_target_pairs={{0,1},{1,0},{2,3},{3,2},{4,5},{5,4},{6,7},{7,6},{8,9},{9,8},{10,11... | collective-permute-start | bytes 98312 | tf_op jit(solution)/shard_map/ppermute | solution.py:309
  308.3 77.3 %collective-permute-start.57 = (f32[32,256]{1,0:T(8,128)}, f32[32,256]{1,0:T(8,128)}, u32[]{:S(2)}, u32[]{:S(2)}) collective-permute-start(f32[32,256]{1,0:T(8,128)} %get-tuple-element.224), channel_id=1, source_target_pairs={{1,2},{2,1},{3,4},{4,3},{5,6},{6,5},{7,8},{8,7},{9,10},{10,9},{11,... | collective-permute-start | bytes 98312 | tf_op jit(solution)/shard_map/ppermute | solution.py:308
  392.5 10.4 %collective-permute-start.58 = (f32[32,256]{1,0:T(8,128)}, f32[32,256]{1,0:T(8,128)}, u32[]{:S(2)}, u32[]{:S(2)}) collective-permute-start(f32[32,256]{1,0:T(8,128)} %get-tuple-element.227), channel_id=1, source_target_pairs={{0,1},{1,0},{2,3},{3,2},{4,5},{5,4},{6,7},{7,6},{8,9},{9,8},{10,11... | collective-permute-start | bytes 98312 | tf_op jit(solution)/shard_map/ppermute | solution.py:309
  392.5 10.4 %collective-permute-start.59 = (f32[32,256]{1,0:T(8,128)}, f32[32,256]{1,0:T(8,128)}, u32[]{:S(2)}, u32[]{:S(2)}) collective-permute-start(f32[32,256]{1,0:T(8,128)} %get-tuple-element.228), channel_id=1, source_target_pairs={{1,2},{2,1},{3,4},{4,3},{5,6},{6,5},{7,8},{8,7},{9,10},{10,9},{11,... | collective-permute-start | bytes 98312 | tf_op jit(solution)/shard_map/ppermute | solution.py:308
  408.5 5.8 collective-permute-start.60
  408.5 9.4 %collective-permute-start.61 = (f32[32,256]{1,0:T(8,128)S(1)}, f32[32,256]{1,0:T(8,128)S(1)}, u32[]{:S(2)}, u32[]{:S(2)}) collective-permute-start(f32[32,256]{1,0:T(8,128)S(1)} %get-tuple-element.232), channel_id=1, source_target_pairs={{1,2},{2,1},{3,4},{4,3},{5,6},{6,5},{7,8},{8,7},{9,10},{10,9},{11,... | collective-permute-start | bytes 98312 | tf_op jit(solution)/shard_map/ppermute | solution.py:308
  422.5 5.7 collective-permute-start.62
  422.5 9.4 %collective-permute-start.63 = (f32[32,256]{1,0:T(8,128)S(1)}, f32[32,256]{1,0:T(8,128)S(1)}, u32[]{:S(2)}, u32[]{:S(2)}) collective-permute-start(f32[32,256]{1,0:T(8,128)S(1)} %get-tuple-element.236), channel_id=1, source_target_pairs={{1,2},{2,1},{3,4},{4,3},{5,6},{6,5},{7,8},{8,7},{9,10},{10,9},{11,... | collective-permute-start | bytes 98312 | tf_op jit(solution)/shard_map/ppermute | solution.py:308
  437.8 10.7 %collective-permute-start.64 = (f32[32,256]{1,0:T(8,128)}, f32[32,256]{1,0:T(8,128)}, u32[]{:S(2)}, u32[]{:S(2)}) collective-permute-start(f32[32,256]{1,0:T(8,128)} %get-tuple-element.239), channel_id=1, source_target_pairs={{0,1},{1,0},{2,3},{3,2},{4,5},{5,4},{6,7},{7,6},{8,9},{9,8},{10,11... | collective-permute-start | bytes 98312 | tf_op jit(solution)/shard_map/ppermute | solution.py:309
  437.8 10.7 %collective-permute-start.65 = (f32[32,256]{1,0:T(8,128)}, f32[32,256]{1,0:T(8,128)}, u32[]{:S(2)}, u32[]{:S(2)}) collective-permute-start(f32[32,256]{1,0:T(8,128)} %get-tuple-element.240), channel_id=1, source_target_pairs={{1,2},{2,1},{3,4},{4,3},{5,6},{6,5},{7,8},{8,7},{9,10},{10,9},{11,... | collective-permute-start | bytes 98312 | tf_op jit(solution)/shard_map/ppermute | solution.py:308
  452.2 5.7 collective-permute-start.66
  452.3 9.4 %collective-permute-start.67 = (f32[32,256]{1,0:T(8,128)S(1)}, f32[32,256]{1,0:T(8,128)S(1)}, u32[]{:S(2)}, u32[]{:S(2)}) collective-permute-start(f32[32,256]{1,0:T(8,128)S(1)} %get-tuple-element.244), channel_id=1, source_target_pairs={{1,2},{2,1},{3,4},{4,3},{5,6},{6,5},{7,8},{8,7},{9,10},{10,9},{11,... | collective-permute-start | bytes 98312 | tf_op jit(solution)/shard_map/ppermute | solution.py:308
  463.8 6.5 %collective-permute-start.68 = (f32[32,256]{1,0:T(8,128)S(1)}, f32[32,256]{1,0:T(8,128)S(1)}, u32[]{:S(2)}, u32[]{:S(2)}) collective-permute-start(f32[32,256]{1,0:T(8,128)S(1)} %get-tuple-element.247), channel_id=1, source_target_pairs={{0,1},{1,0},{2,3},{3,2},{4,5},{5,4},{6,7},{7,6},{8,9},{9,8},{10,11... | collective-permute-start | bytes 98312 | tf_op jit(solution)/shard_map/ppermute | solution.py:309
  463.9 9.5 %collective-permute-start.69 = (f32[32,256]{1,0:T(8,128)S(1)}, f32[32,256]{1,0:T(8,128)S(1)}, u32[]{:S(2)}, u32[]{:S(2)}) collective-permute-start(f32[32,256]{1,0:T(8,128)S(1)} %get-tuple-element.248), channel_id=1, source_target_pairs={{1,2},{2,1},{3,4},{4,3},{5,6},{6,5},{7,8},{8,7},{9,10},{10,9},{11,... | collective-permute-start | bytes 98312 | tf_op jit(solution)/shard_map/ppermute | solution.py:308
  475.8 70.4 %collective-permute-start.70 = (f32[32,256]{1,0:T(8,128)}, f32[32,256]{1,0:T(8,128)}, u32[]{:S(2)}, u32[]{:S(2)}) collective-permute-start(f32[32,256]{1,0:T(8,128)} %get-tuple-element.250), channel_id=1, source_target_pairs={{0,1},{1,0},{2,3},{3,2},{4,5},{5,4},{6,7},{7,6},{8,9},{9,8},{10,11... | collective-permute-start | bytes 98312 | tf_op jit(solution)/shard_map/ppermute | solution.py:309
  475.8 70.4 %collective-permute-start.71 = (f32[32,256]{1,0:T(8,128)}, f32[32,256]{1,0:T(8,128)}, u32[]{:S(2)}, u32[]{:S(2)}) collective-permute-start(f32[32,256]{1,0:T(8,128)} %get-tuple-element.251), channel_id=1, source_target_pairs={{1,2},{2,1},{3,4},{4,3},{5,6},{6,5},{7,8},{8,7},{9,10},{10,9},{11,... | collective-permute-start | bytes 98312 | tf_op jit(solution)/shard_map/ppermute | solution.py:308
  552.2 11.3 %collective-permute-start.72 = (f32[32,256]{1,0:T(8,128)}, f32[32,256]{1,0:T(8,128)S(1)}, u32[]{:S(2)}, u32[]{:S(2)}) collective-permute-start(f32[32,256]{1,0:T(8,128)} %get-tuple-element.253), channel_id=1, source_target_pairs={{0,1},{1,0},{2,3},{3,2},{4,5},{5,4},{6,7},{7,6},{8,9},{9,8},{10,11... | collective-permute-start | bytes 98312 | tf_op jit(solution)/shard_map/ppermute | solution.py:309
  553.5 10.7 %collective-permute-start.73 = (f32[32,256]{1,0:T(8,128)}, f32[32,256]{1,0:T(8,128)S(1)}, u32[]{:S(2)}, u32[]{:S(2)}) collective-permute-start(f32[32,256]{1,0:T(8,128)} %get-tuple-element.254), channel_id=1, source_target_pairs={{1,2},{2,1},{3,4},{4,3},{5,6},{6,5},{7,8},{8,7},{9,10},{10,9},{11,... | collective-permute-start | bytes 98312 | tf_op jit(solution)/shard_map/ppermute | solution.py:308
  571.7 6.0 collective-permute-start.74
  571.8 9.4 %collective-permute-start.75 = (f32[32,256]{1,0:T(8,128)S(1)}, f32[32,256]{1,0:T(8,128)S(1)}, u32[]{:S(2)}, u32[]{:S(2)}) collective-permute-start(f32[32,256]{1,0:T(8,128)S(1)} %get-tuple-element.257), channel_id=1, source_target_pairs={{1,2},{2,1},{3,4},{4,3},{5,6},{6,5},{7,8},{8,7},{9,10},{10,9},{11,... | collective-permute-start | bytes 98312 | tf_op jit(solution)/shard_map/ppermute | solution.py:308
  584.9 6.0 collective-permute-start.76
  584.9 9.6 %collective-permute-start.77 = (f32[32,256]{1,0:T(8,128)S(1)}, f32[32,256]{1,0:T(8,128)S(1)}, u32[]{:S(2)}, u32[]{:S(2)}) collective-permute-start(f32[32,256]{1,0:T(8,128)S(1)} %get-tuple-element.260), channel_id=1, source_target_pairs={{1,2},{2,1},{3,4},{4,3},{5,6},{6,5},{7,8},{8,7},{9,10},{10,9},{11,... | collective-permute-start | bytes 98312 | tf_op jit(solution)/shard_map/ppermute | solution.py:308
  597.8 9.0 %collective-permute-start.78 = (f32[32,256]{1,0:T(8,128)}, f32[32,256]{1,0:T(8,128)S(1)}, u32[]{:S(2)}, u32[]{:S(2)}) collective-permute-start(f32[32,256]{1,0:T(8,128)} %get-tuple-element.262), channel_id=1, source_target_pairs={{0,1},{1,0},{2,3},{3,2},{4,5},{5,4},{6,7},{7,6},{8,9},{9,8},{10,11... | collective-permute-start | bytes 98312 | tf_op jit(solution)/shard_map/ppermute | solution.py:309
  597.8 9.7 %collective-permute-start.79 = (f32[32,256]{1,0:T(8,128)}, f32[32,256]{1,0:T(8,128)S(1)}, u32[]{:S(2)}, u32[]{:S(2)}) collective-permute-start(f32[32,256]{1,0:T(8,128)} %get-tuple-element.263), channel_id=1, source_target_pairs={{1,2},{2,1},{3,4},{4,3},{5,6},{6,5},{7,8},{8,7},{9,10},{10,9},{11,... | collective-permute-start | bytes 98312 | tf_op jit(solution)/shard_map/ppermute | solution.py:308
  610.4 5.5 collective-permute-start.80
  610.5 9.5 %collective-permute-start.81 = (f32[32,256]{1,0:T(8,128)S(1)}, f32[32,256]{1,0:T(8,128)S(1)}, u32[]{:S(2)}, u32[]{:S(2)}) collective-permute-start(f32[32,256]{1,0:T(8,128)S(1)} %get-tuple-element.266), channel_id=1, source_target_pairs={{1,2},{2,1},{3,4},{4,3},{5,6},{6,5},{7,8},{8,7},{9,10},{10,9},{11,... | collective-permute-start | bytes 98312 | tf_op jit(solution)/shard_map/ppermute | solution.py:308
  622.0 8.5 %collective-permute-start.82 = (f32[32,256]{1,0:T(8,128)S(1)}, f32[32,256]{1,0:T(8,128)S(1)}, u32[]{:S(2)}, u32[]{:S(2)}) collective-permute-start(f32[32,256]{1,0:T(8,128)S(1)} %get-tuple-element.268), channel_id=1, source_target_pairs={{0,1},{1,0},{2,3},{3,2},{4,5},{5,4},{6,7},{7,6},{8,9},{9,8},{10,11... | collective-permute-start | bytes 98312 | tf_op jit(solution)/shard_map/ppermute | solution.py:309
  622.1 9.5 %collective-permute-start.83 = (f32[32,256]{1,0:T(8,128)S(1)}, f32[32,256]{1,0:T(8,128)S(1)}, u32[]{:S(2)}, u32[]{:S(2)}) collective-permute-start(f32[32,256]{1,0:T(8,128)S(1)} %get-tuple-element.269), channel_id=1, source_target_pairs={{1,2},{2,1},{3,4},{4,3},{5,6},{6,5},{7,8},{8,7},{9,10},{10,9},{11,... | collective-permute-start | bytes 98312 | tf_op jit(solution)/shard_map/ppermute | solution.py:308
  (107 other events, 4142.0 us)
